TPU v7x, 512 devices: a whole 4x8x8 slice. The times are simulated.
512 devices in a mesh: date: 64 (over y, x, core), pix: 8 (over z).
Axes of the slice: x: 4, y: 8, z: 8, core: 2. Of those that a mesh axis runs over, the one named last changes fastest.
Arguments:
- scene_groups: bfloat16 [512, 64, 4, 2, 16, 128], P(('date', 'pix')), may hold values from -12 to 12
- epoch_interpolator_weights: float32 [512, 8], P(('date', 'pix')), may hold values from -2.4 to 2.4
- epoch_group_numbers: int32 [512, 64], P(('date', 'pix')), may hold values from 0 to 4, as said below
- group_patch_places: int32 [512, 64, 4], P(('date', 'pix')), may hold values from 0 to 7, as said below
- epoch_couples: int32 [1200, 2], replicated, may hold values from 0 to 511, as said below
Outputs:
- displacement: float32 [512, 262144], P(None, ('date', 'pix'))
Inputs may be any that keep to these rules, and one draw needn't show every extreme that they name: `epoch_group_numbers`: a date holds 4 blocks for some tiles in every draw. `group_patch_places`: the 4 entries of one date and tile are distinct slots; entries at or beyond the count are not used. epoch_couples[k, 0] < epoch_couples[k, 1] <= epoch_couples[k, 0] + 8; some pair spans 8 dates and ends at the last date.
All inputs are finite; a program needn't handle non-finite values.
Results may differ from a plain program's by a relative error of at most 0.0073.
Values may be sent and summed in bfloat16 or wider, within the bound.
A program may use at most 128 MiB of HBM per device.

v0:
```python
import jax
import jax.numpy as jnp
from jax import lax
from jax.experimental import pallas as pl
from jax.experimental.pallas import tpu as pltpu
from jax.sharding import PartitionSpec as P

ALONG_TRACK_LINES = 128
LOOKS = 4
TAPS = 8
GROUPS = 4
SLOTS = 8
PAIRS = 1200
DATES = 512
HALF = 608
PADDED = 2 * HALF
BLOCKS = 64
TILES = 64
HALF_TILES = 32
N_PIX = 8
CHUNK = 8
BATCH = 16
EARLY_LEVELS = 3
VMEM_BYTES = 56 * 1024 * 1024
MESH = pl.DeviceIdType.MESH
f32 = jnp.float32
bf16 = jnp.bfloat16
HIGHEST = lax.Precision.HIGHEST


def iota(shape, dim):
    return lax.broadcasted_iota(jnp.int32, shape, dim)


def dot(a, b):
    return jnp.dot(a, b, preferred_element_type=f32)


def split2(x):
    high = x.astype(bf16)
    low = (x - high.astype(f32)).astype(bf16)
    return high, low


def build_row_matrix(w_ref, e_ref):
    lane = iota((128, 128), 1)
    lag = iota((128, 128), 0) - 4 * (lane % 32) + TAPS // 2
    for j in range(LOOKS):
        taps = jnp.zeros((128, 128), f32)
        for tap in range(TAPS):
            taps = jnp.where(lag - j == tap, w_ref[0, tap], taps)
        for g in range(4):
            e_ref[g * 128 : (g + 1) * 128, j * 128 : (j + 1) * 128] = jnp.where(
                lane // 32 == g, taps, 0.0
            ).astype(bf16)


def resample(x_ref, w_ref, e_ref, spread_ref, o_ref):
    build_row_matrix(w_ref, e_ref)
    row = iota((128, 128), 0)
    column = iota((128, 128), 1)
    source = (row % 4) * 32 + (row // 64) * 16 + (row // 4 % 8) * 2 + row // 32 % 2
    pick = jnp.where(source == column, 1.0, 0.0).astype(bf16)

    def one_chunk(step, carry):
        parts = []
        for k in range(CHUNK):
            at = pl.multiple_of((step * CHUNK + k) * 128, 128)
            g = dot(pick, x_ref[pl.ds(at, 128), :]).astype(bf16)
            parts.append(
                jnp.concatenate([g[32 * q : 32 * (q + 1)] for q in range(4)], axis=1)
            )
        lhs = jnp.concatenate(parts, axis=0)
        y = dot(lhs, e_ref[...])
        rows = CHUNK * 32
        for j in range(LOOKS):
            spread_ref[pl.ds(j, rows, stride=LOOKS), :] = y[:, j * 128 : (j + 1) * 128]
        for k in range(CHUNK // 2):
            u = step * (CHUNK // 2) + k
            o_ref[u] = (
                spread_ref[k * 256 : (k + 1) * 256, :].astype(bf16).reshape(2, 8, 16, 128)
            )
        return carry

    lax.fori_loop(0, TILES // CHUNK, one_chunk, 0)


def block_inverse(rows):
    sub = iota((8, 128), 0)
    rows = list(rows)
    for k in range(8):
        inverse = 1.0 / rows[k][k : k + 1, :]
        pivot = jnp.where(sub == k, inverse, rows[k] * inverse)
        for r in range(8):
            if r != k:
                rows[r] = jnp.where(sub == k, 0.0, rows[r]) - rows[r][k : k + 1, :] * pivot
        rows[k] = pivot
    return rows


def block_product(a, b):
    out = []
    for r in range(8):
        total = a[r][0:1, :] * b[0]
        for k in range(1, 8):
            total = total + a[r][k : k + 1, :] * b[k]
        out.append(total)
    return out


def shifted(rows, amount):
    return [pltpu.roll(x, amount, 1) for x in rows]


def joined(rows):
    lane = iota((8, 128), 1)
    return jnp.concatenate(
        [
            jnp.where(lane < 64, rows[2 * q], pltpu.roll(rows[2 * q + 1], 64, 1))
            for q in range(4)
        ],
        axis=1,
    )


def normal_parts(couples_ref, design_ref):
    position = iota((DATES, PADDED), 0)
    date = (position % BLOCKS) * 8 + position // BLOCKS
    later = jnp.where(date == couples_ref[1:2, :], 1.0, 0.0)
    earlier = jnp.where(date == couples_ref[0:1, :], 1.0, 0.0)
    design_ref[...] = (later - earlier).astype(bf16)
    lane = iota((BLOCKS, 512), 1)
    offset = iota((BLOCKS, 512), 0) - lane % BLOCKS
    parts = {-1: [], 0: [], 1: []}
    for c in range(8):
        rows = lax.dot_general(
            design_ref[c * 64 : (c + 1) * 64, :],
            design_ref[...],
            (((1,), (1,)), ((), ())),
            preferred_element_type=f32,
        )
        rows = rows + jnp.where((offset == 0) & (lane // BLOCKS == c), 1.0, 0.0)
        for at in parts:
            parts[at].append(
                jnp.sum(jnp.where(offset == at, rows, 0.0), axis=0, keepdims=True)
            )
    small = iota((8, 128), 1)
    sub = iota((8, 128), 0)
    out = []
    for at in (-1, 0, 1):
        whole = jnp.concatenate(parts[at], axis=0)
        rows = []
        for r in range(8):
            x = whole[:, (r // 2) * 128 : (r // 2 + 1) * 128]
            if r % 2:
                x = pltpu.roll(x, 64, 1)
            pad = jnp.where(sub == r, 1.0, 0.0) if at == 0 else jnp.zeros((8, 128), f32)
            rows.append(jnp.where(small < 64, x, pad))
        out.append(tuple(rows))
    return tuple(out)


def write_factor(factor_ref, before, at, after, hop):
    lane = iota((BLOCKS, 512), 1)
    offset = iota((BLOCKS, 512), 0) - lane % BLOCKS
    for c in range(8):
        x = jnp.where(offset == 0, at[c : c + 1, :], 0.0)
        if before is not None:
            x = jnp.where(offset == -hop, before[c : c + 1, :], x)
            x = jnp.where(offset == hop, after[c : c + 1, :], x)
        factor_ref[c * 64 : (c + 1) * 64, :] = x


def times_factor(left_ref, factor_ref):
    def one_block(step, carry):
        at = pl.multiple_of(step * 128, 128)
        rows = pl.ds(at, 128)
        left_ref[rows, :] = jnp.dot(
            left_ref[rows, :], factor_ref[...], preferred_element_type=f32, precision=HIGHEST
        )
        return carry

    lax.fori_loop(0, 4, one_block, 0)


def reduce_levels(parts, left_ref, factor_ref, levels, first):
    lane512 = iota((8, 512), 1)
    unit = jnp.where(iota((8, 512), 0) == lane512 // BLOCKS, 1.0, 0.0)

    def one_level(level, carry):
        low, mid, up = carry
        hop = jnp.left_shift(1, level)
        back = 128 - hop
        inverse = block_inverse(mid)
        alpha = [-x for x in block_product(low, shifted(inverse, hop))]
        gamma = [-x for x in block_product(up, shifted(inverse, back))]
        write_factor(factor_ref, joined(alpha), unit, joined(gamma), hop)
        add_low = block_product(alpha, shifted(up, hop))
        add_up = block_product(gamma, shifted(low, back))
        mid = tuple(m + a + b for m, a, b in zip(mid, add_low, add_up))
        new_low = tuple(block_product(alpha, shifted(low, hop)))
        new_up = tuple(block_product(gamma, shifted(up, back)))
        times_factor(left_ref, factor_ref)
        return new_low, mid, new_up

    return lax.fori_loop(first, first + levels, one_level, parts)


def start_left(left_ref):
    left_ref[...] = jnp.where(
        iota((DATES, DATES), 0) == iota((DATES, DATES), 1), 1.0, 0.0
    )


def finish_operator(parts, left_ref, factor_ref, terms_ref, design_ref, high_ref, low_ref):
    inverse = joined(block_inverse(parts[1]))
    write_factor(factor_ref, None, inverse, None, 0)
    times_factor(left_ref, factor_ref)
    x = left_ref[...]
    x1, x2 = split2(x)
    terms_ref[0] = x1
    terms_ref[1] = x2
    terms_ref[2] = (x - x1.astype(f32) - x2.astype(f32)).astype(bf16)

    def one_block(step, carry):
        at = pl.multiple_of(step * 128, 128)
        date = iota((128, DATES), 0) + at
        position = iota((128, DATES), 1)
        order = jnp.where(
            (position % BLOCKS) * 8 + position // BLOCKS == date, 1.0, 0.0
        ).astype(bf16)
        m = jnp.zeros((128, PADDED), f32)
        for term in (2, 1, 0):
            m = m + dot(dot(order, terms_ref[term]).astype(bf16), design_ref[...])
        high, low = split2(m)
        high_ref[pl.ds(at, 128), :] = high
        low_ref[pl.ds(at, 128), :] = low
        return carry

    lax.fori_loop(0, DATES // 128, one_block, 0)


def exchange_kernel(
    x_ref, w_ref, couples_ref, own_codes_ref,
    landed_ref, high_ref, low_ref, codes_ref,
    c_mid, c_sum, c_all,
    e_ref, spread_ref, o_ref, z_mid, d_mid, design_ref, left_ref, factor_ref, terms_ref,
    send_z1, recv_z1, send_d1, recv_d1, send_d2, recv_d2, send_z2, recv_z2, local_sem,
    send_c1, recv_c1, send_c2, recv_c2,
):
    a = lax.axis_index("date")
    z = lax.axis_index("pix")
    core = lax.rem(a, 2)
    other = 1 - core
    u = lax.div(a, 2)

    def z_of(step):
        return lax.rem(z + step, N_PIX)

    def u_of(step):
        return lax.rem(u + step, HALF_TILES)

    barrier = pltpu.get_barrier_semaphore()

    def greet(device):
        pl.semaphore_signal(barrier, inc=1, device_id=device, device_id_type=MESH)

    def greet_pix(step, carry):
        greet((a, z_of(step)))
        return carry

    def greet_same(step, carry):
        greet((2 * u_of(step) + core, z))
        return carry

    def greet_other(step, carry):
        greet((2 * u_of(step) + other, z))
        return carry

    lax.fori_loop(1, N_PIX, greet_pix, 0)
    lax.fori_loop(1, HALF_TILES, greet_same, 0)
    lax.fori_loop(0, HALF_TILES, greet_other, 0)

    resample(x_ref, w_ref, e_ref, spread_ref, o_ref)

    pl.semaphore_wait(barrier, N_PIX - 1 + HALF_TILES - 1 + HALF_TILES)

    def pix_first(step):
        to = z_of(step)
        return pltpu.make_async_remote_copy(
            src_ref=o_ref.at[:, core, to], dst_ref=z_mid.at[z],
            send_sem=send_z1.at[step], recv_sem=recv_z1.at[step],
            device_id=(a, to), device_id_type=MESH,
        )

    def date_first(step):
        to = u_of(step)
        return pltpu.make_async_remote_copy(
            src_ref=o_ref.at[to, other], dst_ref=d_mid.at[u],
            send_sem=send_d1.at[step], recv_sem=recv_d1.at[step],
            device_id=(2 * to + other, z), device_id_type=MESH,
        )

    def date_second(step):
        to = u_of(step)
        return pltpu.make_async_remote_copy(
            src_ref=z_mid.at[:, to], dst_ref=landed_ref.at[u, core],
            send_sem=send_d2.at[step], recv_sem=recv_d2.at[step],
            device_id=(2 * to + core, z), device_id_type=MESH,
        )

    def pix_second(step):
        to = z_of(step)
        return pltpu.make_async_remote_copy(
            src_ref=d_mid.at[:, to], dst_ref=landed_ref.at[:, other, z],
            send_sem=send_z2.at[step], recv_sem=recv_z2.at[step],
            device_id=(a, to), device_id_type=MESH,
        )

    def arrival_pix_first(step):
        at = lax.rem(z + N_PIX - step, N_PIX)
        return pltpu.make_async_remote_copy(
            src_ref=o_ref.at[:, core, at], dst_ref=z_mid.at[at],
            send_sem=send_z1.at[step], recv_sem=recv_z1.at[step],
            device_id=(a, at), device_id_type=MESH,
        )

    def arrival_date_first(step):
        at = lax.rem(u + HALF_TILES - step, HALF_TILES)
        return pltpu.make_async_remote_copy(
            src_ref=o_ref.at[at, other], dst_ref=d_mid.at[at],
            send_sem=send_d1.at[step], recv_sem=recv_d1.at[step],
            device_id=(2 * at + other, z), device_id_type=MESH,
        )

    def arrival_date_second(step):
        at = lax.rem(u + HALF_TILES - step, HALF_TILES)
        return pltpu.make_async_remote_copy(
            src_ref=z_mid.at[:, at], dst_ref=landed_ref.at[at, core],
            send_sem=send_d2.at[step], recv_sem=recv_d2.at[step],
            device_id=(2 * at + core, z), device_id_type=MESH,
        )

    def arrival_pix_second(step):
        at = lax.rem(z + N_PIX - step, N_PIX)
        return pltpu.make_async_remote_copy(
            src_ref=d_mid.at[:, at], dst_ref=landed_ref.at[:, other, at],
            send_sem=send_z2.at[step], recv_sem=recv_z2.at[step],
            device_id=(a, at), device_id_type=MESH,
        )

    def code_to_other(step):
        to = 2 * u_of(step) + other
        return pltpu.make_async_remote_copy(
            src_ref=own_codes_ref.at[to], dst_ref=c_mid.at[a],
            send_sem=send_c1.at[step], recv_sem=recv_c1.at[step],
            device_id=(to, z), device_id_type=MESH,
        )

    def code_to_same(step):
        to = 2 * u_of(step) + core
        return pltpu.make_async_remote_copy(
            src_ref=own_codes_ref.at[to], dst_ref=c_mid.at[a],
            send_sem=send_c1.at[HALF_TILES + step], recv_sem=recv_c1.at[HALF_TILES + step],
            device_id=(to, z), device_id_type=MESH,
        )

    def arrival_code_other(step):
        at = 2 * lax.rem(u + HALF_TILES - step, HALF_TILES) + other
        return pltpu.make_async_remote_copy(
            src_ref=own_codes_ref.at[at], dst_ref=c_mid.at[at],
            send_sem=send_c1.at[step], recv_sem=recv_c1.at[step],
            device_id=(at, z), device_id_type=MESH,
        )

    def arrival_code_same(step):
        at = 2 * lax.rem(u + HALF_TILES - step, HALF_TILES) + core
        return pltpu.make_async_remote_copy(
            src_ref=own_codes_ref.at[at], dst_ref=c_mid.at[at],
            send_sem=send_c1.at[HALF_TILES + step], recv_sem=recv_c1.at[HALF_TILES + step],
            device_id=(at, z), device_id_type=MESH,
        )

    def code_second(step):
        to = z_of(step)
        return pltpu.make_async_remote_copy(
            src_ref=c_sum, dst_ref=c_all.at[z],
            send_sem=send_c2.at[step], recv_sem=recv_c2.at[step],
            device_id=(a, to), device_id_type=MESH,
        )

    def arrival_code_second(step):
        at = lax.rem(z + N_PIX - step, N_PIX)
        return pltpu.make_async_remote_copy(
            src_ref=c_sum, dst_ref=c_all.at[at],
            send_sem=send_c2.at[step], recv_sem=recv_c2.at[step],
            device_id=(a, at), device_id_type=MESH,
        )

    def each(first, last, act):
        def body(step, carry):
            act(step)
            return carry

        lax.fori_loop(first, last, body, 0)

    each(1, N_PIX, lambda s: pix_first(s).start())
    each(0, HALF_TILES, lambda s: date_first(s).start())
    own_first = pltpu.make_async_copy(o_ref.at[:, core, z], z_mid.at[z], local_sem.at[0])
    own_first.start()
    each(0, HALF_TILES, lambda s: code_to_other(s).start())
    each(1, HALF_TILES, lambda s: code_to_same(s).start())
    c_mid[a] = own_codes_ref[a]

    parts = normal_parts(couples_ref, design_ref)
    start_left(left_ref)
    parts = reduce_levels(parts, left_ref, factor_ref, EARLY_LEVELS, 0)

    each(0, HALF_TILES, lambda s: arrival_code_other(s).wait_recv())
    each(1, HALF_TILES, lambda s: arrival_code_same(s).wait_recv())
    for p in range(8):
        c_sum[p : p + 1, :] = jnp.sum(c_mid[8 * p : 8 * (p + 1)], axis=0)
    c_all[z] = c_sum[...]
    each(1, N_PIX, lambda s: code_second(s).start())

    own_first.wait()
    each(1, N_PIX, lambda s: arrival_pix_first(s).wait_recv())
    each(1, HALF_TILES, lambda s: date_second(s).start())
    own_date = pltpu.make_async_copy(
        z_mid.at[:, u], landed_ref.at[u, core], local_sem.at[1]
    )
    own_date.start()
    each(0, HALF_TILES, lambda s: arrival_date_first(s).wait_recv())
    each(1, N_PIX, lambda s: pix_second(s).start())
    own_pix = pltpu.make_async_copy(
        d_mid.at[:, z], landed_ref.at[:, other, z], local_sem.at[2]
    )
    own_pix.start()

    parts = reduce_levels(parts, left_ref, factor_ref, 6 - EARLY_LEVELS, EARLY_LEVELS)
    finish_operator(parts, left_ref, factor_ref, terms_ref, design_ref, high_ref, low_ref)

    own_date.wait()
    own_pix.wait()
    each(1, HALF_TILES, lambda s: arrival_date_second(s).wait_recv())
    each(1, N_PIX, lambda s: arrival_pix_second(s).wait_recv())
    each(1, N_PIX, lambda s: arrival_code_second(s).wait_recv())
    codes_ref[...] = c_all[...]
    each(0, HALF_TILES, lambda s: code_to_other(s).wait_send())
    each(1, HALF_TILES, lambda s: code_to_same(s).wait_send())
    each(1, N_PIX, lambda s: code_second(s).wait_send())
    each(1, N_PIX, lambda s: pix_first(s).wait_send())
    each(0, HALF_TILES, lambda s: date_first(s).wait_send())
    each(1, HALF_TILES, lambda s: date_second(s).wait_send())
    each(1, N_PIX, lambda s: pix_second(s).wait_send())


def exchange(x, w, couples, own_codes):
    vmem = pl.BlockSpec(memory_space=pltpu.VMEM)
    dma = pltpu.SemaphoreType.DMA
    return pl.pallas_call(
        exchange_kernel,
        out_shape=(
            jax.ShapeDtypeStruct((HALF_TILES, 2, N_PIX, 16, 128), bf16),
            jax.ShapeDtypeStruct((DATES, PADDED), bf16),
            jax.ShapeDtypeStruct((DATES, PADDED), bf16),
            jax.ShapeDtypeStruct((N_PIX, 8, 128), f32),
        ),
        in_specs=[vmem, pl.BlockSpec(memory_space=pltpu.SMEM), vmem, vmem],
        out_specs=(pl.BlockSpec(memory_space=pl.ANY), vmem, vmem, vmem),
        scratch_shapes=[
            pltpu.VMEM((TILES, 1, 128), f32),
            pltpu.VMEM((8, 128), f32),
            pltpu.VMEM((N_PIX, 8, 128), f32),
            pltpu.VMEM((512, 512), bf16),
            pltpu.VMEM((CHUNK * 128, 128), f32),
            pltpu.VMEM((HALF_TILES, 2, N_PIX, 16, 128), bf16),
            pltpu.VMEM((N_PIX, HALF_TILES, 16, 128), bf16),
            pltpu.VMEM((HALF_TILES, N_PIX, 16, 128), bf16),
            pltpu.VMEM((DATES, PADDED), bf16),
            pltpu.VMEM((DATES, DATES), f32),
            pltpu.VMEM((DATES, DATES), f32),
            pltpu.VMEM((3, DATES, DATES), bf16),
            dma((N_PIX,)), dma((N_PIX,)),
            dma((HALF_TILES,)), dma((HALF_TILES,)),
            dma((HALF_TILES,)), dma((HALF_TILES,)),
            dma((N_PIX,)), dma((N_PIX,)),
            dma((3,)),
            dma((2 * HALF_TILES,)), dma((2 * HALF_TILES,)),
            dma((N_PIX,)), dma((N_PIX,)),
        ],
        compiler_params=pltpu.CompilerParams(
            collective_id=0, has_side_effects=True, vmem_limit_bytes=VMEM_BYTES
        ),
        name="exchange",
    )(x, w, couples, own_codes)


def phase_kernel(
    landed_ref, codes_ref, high_ref, low_ref, couples_ref, out_ref,
    stack_ref, swapped_ref, phase_ref,
):
    row = iota((256, 128), 0)
    column = iota((256, 128), 1)
    fits = (row // 32 == column // 16) & (row // 8 % 4 == column % 4)
    slot = jnp.where(fits, row % 8, -1).astype(f32)
    half = iota((128, 128), 1) < 64

    def place(group, carry):
        pix = lax.div(group, 8)
        eighth = lax.rem(group, 8)
        blocks = landed_ref[pl.ds(eighth * 8, 8), pix].reshape(128, 128)
        chooser = jnp.where(slot == codes_ref[pl.ds(group, 1), :], 1.0, 0.0).astype(bf16)
        turned = pltpu.roll(blocks.astype(f32), 64, 1)
        turned = jnp.where(half, -turned, turned).astype(bf16)
        placed = dot(chooser, jnp.concatenate([blocks, turned], axis=1))
        for q in range(8):
            to = pl.ds(pl.multiple_of(((eighth * 8 + q) * 8 + pix) * 32, 32), 32)
            stack_ref[to, :] = placed[q * 32 : (q + 1) * 32, :128]
            swapped_ref[to, :] = placed[q * 32 : (q + 1) * 32, 128:]
        return carry

    lax.fori_loop(0, BLOCKS, place, 0, unroll=8)

    low_half = iota((8, 128), 1) < 64

    def one_pair(k):
        first = pl.multiple_of(couples_ref[0, k] * 32, 32)
        second = pl.multiple_of(couples_ref[1, k] * 32, 32)
        real = imag = None
        for j in range(LOOKS):
            earlier = stack_ref[pl.ds(first + 8 * j, 8), :]
            r = earlier * stack_ref[pl.ds(second + 8 * j, 8), :]
            i = earlier * swapped_ref[pl.ds(second + 8 * j, 8), :]
            real = r if real is None else real + r
            imag = i if imag is None else imag + i
        return real, imag

    def merge(v, w):
        return jnp.where(low_half, v, w) + pltpu.roll(jnp.where(low_half, w, v), 64, 1)

    def pairs(step, carry):
        found = [
            (one_pair(step * BATCH + q), one_pair(step * BATCH + q + HALF))
            for q in range(BATCH)
        ]
        phases = []
        for (r0, i0), (r1, i1) in found:
            real = merge(r0, r1)
            imag = merge(i0, i1)
            power = jnp.maximum(real * real + imag * imag, float(LOOKS * LOOKS))
            phases.append(imag * lax.rsqrt(power))
        to = pl.ds(pl.multiple_of(step * (8 * BATCH), 8 * BATCH), 8 * BATCH)
        phase_ref[to, :] = jnp.concatenate(phases, axis=0)
        return carry

    lax.fori_loop(0, HALF // BATCH, pairs, 0)

    wide = iota((HALF, 128), 1) < 64
    for part in range(2):
        columns = []
        for p in (2 * part, 2 * part + 1):
            a0 = phase_ref[pl.ds(2 * p, HALF, stride=8), :]
            a1 = phase_ref[pl.ds(2 * p + 1, HALF, stride=8), :]
            columns.append(
                jnp.concatenate(
                    [
                        jnp.where(wide, a0, pltpu.roll(a1, 64, 1)),
                        jnp.where(wide, pltpu.roll(a0, 64, 1), a1),
                    ],
                    axis=0,
                )
            )
        high, low = split2(jnp.concatenate(columns, axis=1))
        out_ref[:, part * 256 : (part + 1) * 256] = dot(high_ref[...], high) + (
            dot(high_ref[...], low) + dot(low_ref[...], high)
        )


def solve_phases(landed, codes, high, low, couples):
    vmem = pl.BlockSpec(memory_space=pltpu.VMEM)
    return pl.pallas_call(
        phase_kernel,
        out_shape=jax.ShapeDtypeStruct((DATES, 512), f32),
        in_specs=[vmem, vmem, vmem, vmem, pl.BlockSpec(memory_space=pltpu.SMEM)],
        out_specs=vmem,
        scratch_shapes=[
            pltpu.VMEM((DATES * 32, 128), f32),
            pltpu.VMEM((DATES * 32, 128), f32),
            pltpu.VMEM((HALF * 8, 128), f32),
        ],
        compiler_params=pltpu.CompilerParams(vmem_limit_bytes=VMEM_BYTES),
        name="phases",
    )(landed, codes, high, low, couples)


def local(scene_groups, weights, numbers, places, couples):
    in_use = jnp.arange(GROUPS, dtype=jnp.int32)[None, :] < numbers[0][:, None]
    codes = jnp.where(in_use, places[0], SLOTS).astype(bf16)
    group = jnp.arange(GROUPS, dtype=jnp.int32)[:, None]
    lane = jnp.arange(128, dtype=jnp.int32)[None, :]
    eighth = lax.rem(lax.axis_index("date"), 8)
    spread = (lane // LOOKS % GROUPS == group) & (lane // 16 == eighth)
    own_codes = jnp.dot(codes, spread.astype(bf16), preferred_element_type=f32)
    couples = jnp.pad(couples.T, ((0, 0), (0, PADDED - PAIRS)))
    landed, high, low, codes = exchange(
        scene_groups.reshape(TILES * 128, 128), weights, couples,
        own_codes.reshape(TILES, 1, 128),
    )
    return solve_phases(
        landed.reshape(TILES, N_PIX, 16, 128), codes.reshape(BLOCKS, 128), high, low, couples
    )


def solution(mesh):
    in_specs = (
        P(("date", "pix"), None, None, None, None, None),
        P(("date", "pix"), None),
        P(("date", "pix"), None),
        P(("date", "pix"), None, None),
        P(),
    )
    out_specs = P(None, ("date", "pix"))
    return jax.shard_map(local, mesh=mesh, in_specs=in_specs, out_specs=out_specs, check_vma=False)
```

profile of v0, /device:TPU:2, one launch (start us, length us, event | category | flops | bytes accessed | tf_op | source)
XLA Modules:
  0.0 98.6 jit_solution(13980489928211478357)
XLA Ops:
  0.0 1.3 %pad.4.couples_ref = s32[2,1216]{1,0:T(2,128)} pad(s32[2,1200]{1,0:T(2,128)} %bitcast.15, s32[]{:T(128)} %constant.43.clone.1), padding=0_0x0_16 | pad | bytes 19332 | tf_op jit(solution)/shard_map/jit(_pad)/pad | solution.py:605
  1.3 1.5 %fusion.2 = f32[64,128]{1,0:T(8,128)} fusion(s32[1,64,4]{1,2,0:T(4,128)} %param.8, s32[128]{0:T(128)S(1)} %and_select_fusion.1, s32[64]{0:T(128)} %bitcast.16, pred[128]{0:T(512)(128)(4,1)S(1)} %fusion.9), kind=kOutput, calls=%fused_computation.7 | convolution fusion | flops 67328 | bytes 34688 | tf_op jit(solution)/shard_map/dot_general | solution.py:604
  2.8 77.7 %exchange.1 = (bf16[32,2,8,16,128]{4,3,2,1,0:T(8,128)(2,1)}, bf16[512,1216]{1,0:T(8,128)(2,1)}, bf16[512,1216]{1,0:T(8,128)(2,1)}, f32[8,8,128]{2,1,0:T(8,128)}) custom-call(bf16[8192,128]{1,0:T(8,128)(2,1)} %bitcast.11, f32[1,8]{1,0:T(1,128)} %w_ref.1, s32[2,1216]{1,0:T(2,128)} %pad.4.couples_ref, f32[64,1,128]{2,1,0:T(1,128)} %bitcast.13), custom_call_target="tpu_custom_call" | custom-call | tf_op jit(solution)/shard_map/exchange/pallas_call | solution.py:461
  80.5 18.1 %phases.1 = f32[512,512]{1,0:T(8,128)} custom-call(bf16[64,8,16,128]{3,2,1,0:T(8,128)(2,1)} %bitcast.12, f32[64,128]{1,0:T(8,128)} %bitcast.14, bf16[512,1216]{1,0:T(8,128)(2,1)} %get-tuple-element.11.high_ref, bf16[512,1216]{1,0:T(8,128)(2,1)} %get-tuple-element.12.low_ref, s32[2,1216]{1,0:T(2,128)} %pad.4.couples_ref), custom_call_target="tpu_custom_call" | custom-call | tf_op jit(solution)/shard_map/phases/pallas_call | solution.py:582
  (2 shorter events, 0.0 us)
where the time goes:
time: 98.8 us; the launch traced here: 98.6 us
  Pallas kernels  95.8 us (97%)
  matrix products  1.5 us (2%)
  local copies, waits for them, and re-layouts  1.3 us (1%)
    pallas_call x1, Pallas kernels, exchange(): pl.pallas_call(exchange_kernel, out_shape=(jax.ShapeDtypeStruct((HALF_TIL...  77.7 us
    pallas_call x1, Pallas kernels, solve_phases(): pl.pallas_call(phase_kernel, out_shape=jax.ShapeDtypeStruct((DATES, 512),...  18.1 us

commit v1 on v0

v1 whole, which is shorter than its diff:
```python
import jax
import jax.numpy as jnp
from jax import lax
from jax.experimental import pallas as pl
from jax.experimental.pallas import tpu as pltpu
from jax.sharding import PartitionSpec as P

ALONG_TRACK_LINES = 128
LOOKS = 4
TAPS = 8
GROUPS = 4
SLOTS = 8
PAIRS = 1200
DATES = 512
HALF = PAIRS // 2
BLOCKS = 64
TILES = 64
HALF_TILES = 32
N_PIX = 8
CHUNK = 8
BATCH = 40
EARLY_LEVELS = 3
VMEM_BYTES = 56 * 1024 * 1024
MESH = pl.DeviceIdType.MESH
f32 = jnp.float32
bf16 = jnp.bfloat16
HIGHEST = lax.Precision.HIGHEST


def iota(shape, dim):
    return lax.broadcasted_iota(jnp.int32, shape, dim)


def dot(a, b):
    return jnp.dot(a, b, preferred_element_type=f32)


def split2(x):
    high = x.astype(bf16)
    low = (x - high.astype(f32)).astype(bf16)
    return high, low


def build_row_matrix(w_ref, e_ref):
    lane = iota((128, 128), 1)
    lag = iota((128, 128), 0) - 4 * (lane % 32) + TAPS // 2
    for j in range(LOOKS):
        taps = jnp.zeros((128, 128), f32)
        for tap in range(TAPS):
            taps = jnp.where(lag - j == tap, w_ref[0, tap], taps)
        for g in range(4):
            e_ref[g * 128 : (g + 1) * 128, j * 128 : (j + 1) * 128] = jnp.where(
                lane // 32 == g, taps, 0.0
            ).astype(bf16)


def resample_chunk(at, pick, x_ref, e_ref, spread_ref, o_ref):
    parts = []
    for k in range(CHUNK):
        rows = pl.ds(pl.multiple_of((at * CHUNK + k) * 128, 128), 128)
        g = dot(pick, x_ref[rows, :]).astype(bf16)
        parts.append(jnp.concatenate([g[32 * q : 32 * (q + 1)] for q in range(4)], axis=1))
    y = dot(jnp.concatenate(parts, axis=0), e_ref[...])
    for j in range(LOOKS):
        spread_ref[pl.ds(j, CHUNK * 32, stride=LOOKS), :] = y[:, j * 128 : (j + 1) * 128]
    for k in range(CHUNK // 2):
        o_ref[at * (CHUNK // 2) + k] = (
            spread_ref[k * 256 : (k + 1) * 256, :].astype(bf16).reshape(2, 8, 16, 128)
        )


def row_picker():
    row = iota((128, 128), 0)
    column = iota((128, 128), 1)
    source = (row % 4) * 32 + (row // 64) * 16 + (row // 4 % 8) * 2 + row // 32 % 2
    return jnp.where(source == column, 1.0, 0.0).astype(bf16)


def block_inverse(rows):
    sub = iota((8, 128), 0)
    rows = list(rows)
    for k in range(8):
        inverse = 1.0 / rows[k][k : k + 1, :]
        pivot = jnp.where(sub == k, inverse, rows[k] * inverse)
        for r in range(8):
            if r != k:
                rows[r] = jnp.where(sub == k, 0.0, rows[r]) - rows[r][k : k + 1, :] * pivot
        rows[k] = pivot
    return rows


def block_product(a, b):
    out = []
    for r in range(8):
        total = a[r][0:1, :] * b[0]
        for k in range(1, 8):
            total = total + a[r][k : k + 1, :] * b[k]
        out.append(total)
    return out


def shifted(rows, amount):
    return [pltpu.roll(x, amount, 1) for x in rows]


def joined(rows):
    lane = iota((8, 128), 1)
    return jnp.concatenate(
        [
            jnp.where(lane < 64, rows[2 * q], pltpu.roll(rows[2 * q + 1], 64, 1))
            for q in range(4)
        ],
        axis=1,
    )


def normal_parts(couples_ref, design_ref):
    position = iota((DATES, PAIRS), 0)
    date = (position % BLOCKS) * 8 + position // BLOCKS
    later = jnp.where(date == couples_ref[1:2, :], 1.0, 0.0)
    earlier = jnp.where(date == couples_ref[0:1, :], 1.0, 0.0)
    design_ref[...] = (later - earlier).astype(bf16)
    lane = iota((BLOCKS, 512), 1)
    offset = iota((BLOCKS, 512), 0) - lane % BLOCKS
    parts = {-1: [], 0: [], 1: []}
    for c in range(8):
        rows = lax.dot_general(
            design_ref[c * 64 : (c + 1) * 64, :],
            design_ref[...],
            (((1,), (1,)), ((), ())),
            preferred_element_type=f32,
        )
        rows = rows + jnp.where((offset == 0) & (lane // BLOCKS == c), 1.0, 0.0)
        for at in parts:
            parts[at].append(
                jnp.sum(jnp.where(offset == at, rows, 0.0), axis=0, keepdims=True)
            )
    small = iota((8, 128), 1)
    sub = iota((8, 128), 0)
    out = []
    for at in (-1, 0, 1):
        whole = jnp.concatenate(parts[at], axis=0)
        rows = []
        for r in range(8):
            x = whole[:, (r // 2) * 128 : (r // 2 + 1) * 128]
            if r % 2:
                x = pltpu.roll(x, 64, 1)
            pad = jnp.where(sub == r, 1.0, 0.0) if at == 0 else jnp.zeros((8, 128), f32)
            rows.append(jnp.where(small < 64, x, pad))
        out.append(tuple(rows))
    return tuple(out)


def write_factor(factor_ref, before, at, after, hop):
    lane = iota((BLOCKS, 512), 1)
    offset = iota((BLOCKS, 512), 0) - lane % BLOCKS
    for c in range(8):
        x = jnp.where(offset == 0, at[c : c + 1, :], 0.0)
        if before is not None:
            x = jnp.where(offset == -hop, before[c : c + 1, :], x)
            x = jnp.where(offset == hop, after[c : c + 1, :], x)
        factor_ref[c * 64 : (c + 1) * 64, :] = x


def times_factor(left_ref, factor_ref):
    def one_block(step, carry):
        at = pl.multiple_of(step * 128, 128)
        rows = pl.ds(at, 128)
        left_ref[rows, :] = jnp.dot(
            left_ref[rows, :], factor_ref[...], preferred_element_type=f32, precision=HIGHEST
        )
        return carry

    lax.fori_loop(0, 4, one_block, 0)


def reduce_level(level, parts, write_ref):
    low, mid, up = parts
    unit = jnp.where(iota((8, 512), 0) == iota((8, 512), 1) // BLOCKS, 1.0, 0.0)
    hop = 2**level if isinstance(level, int) else jnp.left_shift(1, level)
    back = 128 - hop
    inverse = block_inverse(mid)
    alpha = [-x for x in block_product(low, shifted(inverse, hop))]
    gamma = [-x for x in block_product(up, shifted(inverse, back))]
    write_factor(write_ref, joined(alpha), unit, joined(gamma), hop)
    add_low = block_product(alpha, shifted(up, hop))
    add_up = block_product(gamma, shifted(low, back))
    mid = tuple(m + a + b for m, a, b in zip(mid, add_low, add_up))
    new_low = tuple(block_product(alpha, shifted(low, hop)))
    new_up = tuple(block_product(gamma, shifted(up, back)))
    return new_low, mid, new_up


def reduce_levels(parts, left_ref, factor_ref, first, last):
    def one_level(level, carry):
        carry = reduce_level(level, carry, factor_ref)
        times_factor(left_ref, factor_ref)
        return carry

    return lax.fori_loop(first, last, one_level, parts)


def finish_operator(parts, left_ref, factor_ref, terms_ref, design_ref, high_ref, low_ref):
    inverse = joined(block_inverse(parts[1]))
    write_factor(factor_ref, None, inverse, None, 0)
    times_factor(left_ref, factor_ref)
    x = left_ref[...]
    x1, x2 = split2(x)
    terms_ref[0] = x1
    terms_ref[1] = x2
    terms_ref[2] = (x - x1.astype(f32) - x2.astype(f32)).astype(bf16)

    def one_block(step, carry):
        at = pl.multiple_of(step * 128, 128)
        date = iota((128, DATES), 0) + at
        position = iota((128, DATES), 1)
        order = jnp.where(
            (position % BLOCKS) * 8 + position // BLOCKS == date, 1.0, 0.0
        ).astype(bf16)
        m = jnp.zeros((128, PAIRS), f32)
        for term in (2, 1, 0):
            m = m + dot(dot(order, terms_ref[term]).astype(bf16), design_ref[...])
        high, low = split2(m)
        high_ref[pl.ds(at, 128), :] = high
        low_ref[pl.ds(at, 128), :] = low
        return carry

    lax.fori_loop(0, DATES // 128, one_block, 0)


def own_code_rows(u, numbers_ref, places_ref, own_codes_ref):
    block = iota((GROUPS, TILES), 0)
    code = jnp.where(block < numbers_ref[...], places_ref[...], SLOTS).astype(f32)
    lane = iota((GROUPS, 128), 1)
    group = iota((GROUPS, 128), 0)
    spread = (lane // LOOKS % GROUPS == group) & (lane // 16 == lax.rem(u, 8))
    rows = lax.dot_general(
        code.astype(bf16),
        jnp.where(spread, 1.0, 0.0).astype(bf16),
        (((0,), (0,)), ((), ())),
        preferred_element_type=f32,
    )
    own_codes_ref[...] = rows.reshape(TILES, 1, 128)


def place_group(slot, pix, parity, part, landed_ref, codes_ref, stack_ref, swapped_ref):
    half = iota((128, 128), 1) < 64
    blocks = landed_ref[part * 8 : (part + 1) * 8, parity, pix].reshape(128, 128)
    row = codes_ref[pix, pl.ds(parity * 4 + part, 1), :]
    chooser = jnp.where(slot == row, 1.0, 0.0).astype(bf16)
    turned = pltpu.roll(blocks.astype(f32), 64, 1)
    turned = jnp.where(half, -turned, turned).astype(bf16)
    placed = dot(chooser, jnp.concatenate([blocks, turned], axis=1))
    for q in range(8):
        date = (2 * (8 * part + q) + parity) * 8 + pix
        stack_ref[date] = placed[q * 32 : (q + 1) * 32, :128]
        swapped_ref[date] = placed[q * 32 : (q + 1) * 32, 128:]


def exchange_kernel(
    x_hbm, w_ref, couples_ref, pairs_ref, numbers_ref, places_ref,
    out_ref,
    x_ref, own_codes_ref, c_mid, c_sum, c_all, landed_ref, high_ref, low_ref,
    stack_ref, swapped_ref, phase_ref,
    e_ref, spread_ref, o_ref, z_mid, d_mid, design_ref, left_ref, factor_ref, terms_ref,
    send_z1, recv_z1, send_d1, recv_d1, send_d2, recv_d2, send_z2, recv_z2, local_sem, x_sem,
    send_c1, recv_c1, send_c2, recv_c2,
):
    a = lax.axis_index("date")
    z = lax.axis_index("pix")
    core = lax.rem(a, 2)
    other = 1 - core
    u = lax.div(a, 2)

    def z_of(step):
        return lax.rem(z + step, N_PIX)

    def u_of(step):
        return lax.rem(u + step, HALF_TILES)

    def chunk_of(step):
        return 4 + (1 - 2 * lax.rem(step, 2)) * lax.div(step + 1, 2)

    def load_chunk(step):
        at = lax.rem(lax.div(u, 4) + chunk_of(step), 8)
        rows = pl.ds(pl.multiple_of(at * 1024, 1024), 1024)
        return pltpu.make_async_copy(x_hbm.at[rows], x_ref.at[rows], x_sem.at[step])

    def each(first, last, act):
        def body(step, carry):
            act(step)
            return carry

        lax.fori_loop(first, last, body, 0)

    each(0, 8, lambda s: load_chunk(s).start())

    barrier = pltpu.get_barrier_semaphore()

    def greet(device):
        pl.semaphore_signal(barrier, inc=1, device_id=device, device_id_type=MESH)

    def greet_pix(step, carry):
        greet((a, z_of(step)))
        return carry

    def greet_same(step, carry):
        greet((2 * u_of(step) + core, z))
        return carry

    def greet_other(step, carry):
        greet((2 * u_of(step) + other, z))
        return carry

    lax.fori_loop(1, N_PIX, greet_pix, 0)
    lax.fori_loop(1, HALF_TILES, greet_same, 0)
    lax.fori_loop(0, HALF_TILES, greet_other, 0)

    build_row_matrix(w_ref, e_ref)
    own_code_rows(u, numbers_ref, places_ref, own_codes_ref)

    pl.semaphore_wait(barrier, N_PIX - 1 + HALF_TILES - 1 + HALF_TILES)

    def pix_first(step):
        to = z_of(step)
        return pltpu.make_async_remote_copy(
            src_ref=o_ref.at[:, core, to], dst_ref=z_mid.at[z],
            send_sem=send_z1.at[step], recv_sem=recv_z1.at[step],
            device_id=(a, to), device_id_type=MESH,
        )

    def pix_first_part(step, at):
        to = z_of(step)
        tiles = pl.ds(at * 4, 4)
        return pltpu.make_async_remote_copy(
            src_ref=o_ref.at[tiles, core, to], dst_ref=z_mid.at[z, tiles],
            send_sem=send_z1.at[step], recv_sem=recv_z1.at[step],
            device_id=(a, to), device_id_type=MESH,
        )

    def tile_near(down, across):
        return lax.rem(lax.div(u, 4) + down, 8) * 4 + lax.rem(u + across, 4)

    def date_first(down, across):
        to = tile_near(down, across)
        return pltpu.make_async_remote_copy(
            src_ref=o_ref.at[to, other], dst_ref=d_mid.at[u],
            send_sem=send_d1.at[down * 4 + across], recv_sem=recv_d1.at[down * 4 + across],
            device_id=(2 * to + other, z), device_id_type=MESH,
        )

    def date_second(step):
        to = u_of(step)
        return pltpu.make_async_remote_copy(
            src_ref=z_mid.at[:, to], dst_ref=landed_ref.at[u, core],
            send_sem=send_d2.at[step], recv_sem=recv_d2.at[step],
            device_id=(2 * to + core, z), device_id_type=MESH,
        )

    def pix_second(step):
        to = z_of(step)
        return pltpu.make_async_remote_copy(
            src_ref=d_mid.at[:, to], dst_ref=landed_ref.at[:, other, z],
            send_sem=send_z2.at[step], recv_sem=recv_z2.at[step],
            device_id=(a, to), device_id_type=MESH,
        )

    def arrival_pix_first(step):
        at = lax.rem(z + N_PIX - step, N_PIX)
        return pltpu.make_async_remote_copy(
            src_ref=o_ref.at[:, core, at], dst_ref=z_mid.at[at],
            send_sem=send_z1.at[step], recv_sem=recv_z1.at[step],
            device_id=(a, at), device_id_type=MESH,
        )

    def arrival_date_first(step):
        down = lax.div(step, 4)
        across = lax.rem(step, 4)
        at = tile_near(8 - down, 4 - across)
        return pltpu.make_async_remote_copy(
            src_ref=o_ref.at[at, other], dst_ref=d_mid.at[at],
            send_sem=send_d1.at[step], recv_sem=recv_d1.at[step],
            device_id=(2 * at + other, z), device_id_type=MESH,
        )

    def arrival_date_second(step):
        at = lax.rem(u + HALF_TILES - step, HALF_TILES)
        return pltpu.make_async_remote_copy(
            src_ref=z_mid.at[:, at], dst_ref=landed_ref.at[at, core],
            send_sem=send_d2.at[step], recv_sem=recv_d2.at[step],
            device_id=(2 * at + core, z), device_id_type=MESH,
        )

    def arrival_pix_second(step):
        at = lax.rem(z + N_PIX - step, N_PIX)
        return pltpu.make_async_remote_copy(
            src_ref=d_mid.at[:, at], dst_ref=landed_ref.at[:, other, at],
            send_sem=send_z2.at[step], recv_sem=recv_z2.at[step],
            device_id=(a, at), device_id_type=MESH,
        )

    def code_to_other(step):
        to = 2 * u_of(step) + other
        return pltpu.make_async_remote_copy(
            src_ref=own_codes_ref.at[to], dst_ref=c_mid.at[a],
            send_sem=send_c1.at[step], recv_sem=recv_c1.at[step],
            device_id=(to, z), device_id_type=MESH,
        )

    def code_to_same(step):
        to = 2 * u_of(step) + core
        return pltpu.make_async_remote_copy(
            src_ref=own_codes_ref.at[to], dst_ref=c_mid.at[a],
            send_sem=send_c1.at[HALF_TILES + step], recv_sem=recv_c1.at[HALF_TILES + step],
            device_id=(to, z), device_id_type=MESH,
        )

    def arrival_code_other(step):
        at = 2 * lax.rem(u + HALF_TILES - step, HALF_TILES) + other
        return pltpu.make_async_remote_copy(
            src_ref=own_codes_ref.at[at], dst_ref=c_mid.at[at],
            send_sem=send_c1.at[step], recv_sem=recv_c1.at[step],
            device_id=(at, z), device_id_type=MESH,
        )

    def arrival_code_same(step):
        at = 2 * lax.rem(u + HALF_TILES - step, HALF_TILES) + core
        return pltpu.make_async_remote_copy(
            src_ref=own_codes_ref.at[at], dst_ref=c_mid.at[at],
            send_sem=send_c1.at[HALF_TILES + step], recv_sem=recv_c1.at[HALF_TILES + step],
            device_id=(at, z), device_id_type=MESH,
        )

    def code_second(step):
        to = z_of(step)
        return pltpu.make_async_remote_copy(
            src_ref=c_sum, dst_ref=c_all.at[z],
            send_sem=send_c2.at[step], recv_sem=recv_c2.at[step],
            device_id=(a, to), device_id_type=MESH,
        )

    def arrival_code_second(step):
        at = lax.rem(z + N_PIX - step, N_PIX)
        return pltpu.make_async_remote_copy(
            src_ref=c_sum, dst_ref=c_all.at[at],
            send_sem=send_c2.at[step], recv_sem=recv_c2.at[step],
            device_id=(a, at), device_id_type=MESH,
        )

    pick = row_picker()

    def send_chunk(step):
        down = chunk_of(step)
        at = lax.rem(lax.div(u, 4) + down, 8)
        load_chunk(step).wait()
        resample_chunk(at, pick, x_ref, e_ref, spread_ref, o_ref)
        for across in range(4):
            date_first(down, across).start()
        each(1, N_PIX, lambda s: pix_first_part(s, at).start())

    each(0, 8, send_chunk)
    own_first = pltpu.make_async_copy(o_ref.at[:, core, z], z_mid.at[z], local_sem.at[0])
    own_first.start()
    each(0, HALF_TILES, lambda s: code_to_other(s).start())
    each(1, HALF_TILES, lambda s: code_to_same(s).start())
    c_mid[a] = own_codes_ref[a]

    parts = normal_parts(couples_ref, design_ref)
    parts = reduce_level(0, parts, left_ref)
    parts = reduce_levels(parts, left_ref, factor_ref, 1, EARLY_LEVELS)

    each(0, HALF_TILES, lambda s: arrival_code_other(s).wait_recv())
    each(1, HALF_TILES, lambda s: arrival_code_same(s).wait_recv())
    for e in range(2):
        for p in range(4):
            total = c_mid[16 * p + e]
            for q in range(1, 8):
                total = total + c_mid[16 * p + 2 * q + e]
            c_sum[4 * e + p : 4 * e + p + 1, :] = total
    c_all[z] = c_sum[...]
    each(1, N_PIX, lambda s: code_second(s).start())

    own_first.wait()
    each(1, N_PIX, lambda s: arrival_pix_first(s).wait_recv())
    each(1, HALF_TILES, lambda s: date_second(s).start())
    own_date = pltpu.make_async_copy(
        z_mid.at[:, u], landed_ref.at[u, core], local_sem.at[1]
    )
    own_date.start()
    each(0, HALF_TILES, lambda s: arrival_date_first(s).wait_recv())
    each(1, N_PIX, lambda s: pix_second(s).start())
    own_pix = pltpu.make_async_copy(
        d_mid.at[:, z], landed_ref.at[:, other, z], local_sem.at[2]
    )
    own_pix.start()

    parts = reduce_levels(parts, left_ref, factor_ref, EARLY_LEVELS, 6)
    finish_operator(parts, left_ref, factor_ref, terms_ref, design_ref, high_ref, low_ref)

    each(1, N_PIX, lambda s: arrival_code_second(s).wait_recv())

    row = iota((256, 128), 0)
    column = iota((256, 128), 1)
    fits = (row // 32 == column // 16) & (row // 8 % 4 == column % 4)
    slot = jnp.where(fits, row % 8, -1).astype(f32)

    def place_pix(pix, parity):
        for part in range(4):
            place_group(slot, pix, parity, part, landed_ref, c_all, stack_ref, swapped_ref)

    def land_pix(step):
        arrival_pix_second(step).wait_recv()
        place_pix(lax.rem(z + N_PIX - step, N_PIX), other)

    own_pix.wait()
    place_pix(z, other)
    each(1, N_PIX, land_pix)
    own_date.wait()
    each(1, HALF_TILES, lambda s: arrival_date_second(s).wait_recv())
    each(0, N_PIX, lambda pix: place_pix(pix, core))

    solve_phases(pairs_ref, high_ref, low_ref, out_ref, stack_ref, swapped_ref, phase_ref)

    each(0, HALF_TILES, lambda s: code_to_other(s).wait_send())
    each(1, HALF_TILES, lambda s: code_to_same(s).wait_send())
    each(1, N_PIX, lambda s: code_second(s).wait_send())
    each(1, N_PIX, lambda s: pix_first(s).wait_send())
    each(0, HALF_TILES, lambda s: date_first(lax.div(s, 4), lax.rem(s, 4)).wait_send())
    each(1, HALF_TILES, lambda s: date_second(s).wait_send())
    each(1, N_PIX, lambda s: pix_second(s).wait_send())


def solve_phases(pairs_ref, high_ref, low_ref, out_ref, stack_ref, swapped_ref, phase_ref):
    low_half = iota((8, 128), 1) < 64

    def one_pair(k):
        earlier = stack_ref[pairs_ref[0, k]]
        later = pairs_ref[1, k]
        real = earlier * stack_ref[later]
        imag = earlier * swapped_ref[later]

        def looks(v):
            return (v[0:8] + v[8:16]) + (v[16:24] + v[24:32])

        return looks(real), looks(imag)

    def merge(v, w):
        return jnp.where(low_half, v, w) + pltpu.roll(jnp.where(low_half, w, v), 64, 1)

    def pairs(step, carry):
        found = [
            (one_pair(step * BATCH + q), one_pair(step * BATCH + q + HALF))
            for q in range(BATCH)
        ]
        phases = []
        for (r0, i0), (r1, i1) in found:
            real = merge(r0, r1)
            imag = merge(i0, i1)
            power = jnp.maximum(real * real + imag * imag, float(LOOKS * LOOKS))
            phases.append(imag * lax.rsqrt(power))
        to = pl.ds(pl.multiple_of(step * (8 * BATCH), 8 * BATCH), 8 * BATCH)
        phase_ref[to, :] = jnp.concatenate(phases, axis=0)
        return carry

    lax.fori_loop(0, HALF // BATCH, pairs, 0)

    wide = iota((HALF, 128), 1) < 64
    for part in range(2):
        columns = []
        for p in (2 * part, 2 * part + 1):
            a0 = phase_ref[pl.ds(2 * p, HALF, stride=8), :]
            a1 = phase_ref[pl.ds(2 * p + 1, HALF, stride=8), :]
            columns.append(
                jnp.concatenate(
                    [
                        jnp.where(wide, a0, pltpu.roll(a1, 64, 1)),
                        jnp.where(wide, pltpu.roll(a0, 64, 1), a1),
                    ],
                    axis=0,
                )
            )
        high, low = split2(jnp.concatenate(columns, axis=1))
        out_ref[:, part * 256 : (part + 1) * 256] = dot(high_ref[...], high) + (
            dot(high_ref[...], low) + dot(low_ref[...], high)
        )


def exchange(x, w, couples, numbers, places):
    vmem = pl.BlockSpec(memory_space=pltpu.VMEM)
    smem = pl.BlockSpec(memory_space=pltpu.SMEM)
    dma = pltpu.SemaphoreType.DMA
    return pl.pallas_call(
        exchange_kernel,
        out_shape=jax.ShapeDtypeStruct((DATES, 512), f32),
        in_specs=[pl.BlockSpec(memory_space=pl.ANY), smem, vmem, smem, vmem, vmem],
        out_specs=vmem,
        scratch_shapes=[
            pltpu.VMEM((TILES * 128, 128), bf16),
            pltpu.VMEM((TILES, 1, 128), f32),
            pltpu.VMEM((TILES, 1, 128), f32),
            pltpu.VMEM((8, 128), f32),
            pltpu.VMEM((N_PIX, 8, 128), f32),
            pltpu.VMEM((HALF_TILES, 2, N_PIX, 16, 128), bf16),
            pltpu.VMEM((DATES, PAIRS), bf16),
            pltpu.VMEM((DATES, PAIRS), bf16),
            pltpu.VMEM((DATES, 32, 128), f32),
            pltpu.VMEM((DATES, 32, 128), f32),
            pltpu.VMEM((HALF * 8, 128), f32),
            pltpu.VMEM((512, 512), bf16),
            pltpu.VMEM((CHUNK * 128, 128), f32),
            pltpu.VMEM((HALF_TILES, 2, N_PIX, 16, 128), bf16),
            pltpu.VMEM((N_PIX, HALF_TILES, 16, 128), bf16),
            pltpu.VMEM((HALF_TILES, N_PIX, 16, 128), bf16),
            pltpu.VMEM((DATES, PAIRS), bf16),
            pltpu.VMEM((DATES, DATES), f32),
            pltpu.VMEM((DATES, DATES), f32),
            pltpu.VMEM((3, DATES, DATES), bf16),
            dma((N_PIX,)), dma((N_PIX,)),
            dma((HALF_TILES,)), dma((HALF_TILES,)),
            dma((HALF_TILES,)), dma((HALF_TILES,)),
            dma((N_PIX,)), dma((N_PIX,)),
            dma((3,)), dma((8,)),
            dma((2 * HALF_TILES,)), dma((2 * HALF_TILES,)),
            dma((N_PIX,)), dma((N_PIX,)),
        ],
        compiler_params=pltpu.CompilerParams(
            collective_id=0, has_side_effects=True, vmem_limit_bytes=VMEM_BYTES
        ),
        name="exchange",
    )(x, w, couples, couples, numbers, places)


def local(scene_groups, weights, numbers, places, couples):
    return exchange(
        scene_groups.reshape(TILES * 128, 128), weights, couples.T, numbers, places[0].T
    )


def solution(mesh):
    in_specs = (
        P(("date", "pix"), None, None, None, None, None),
        P(("date", "pix"), None),
        P(("date", "pix"), None),
        P(("date", "pix"), None, None),
        P(),
    )
    out_specs = P(None, ("date", "pix"))
    return jax.shard_map(local, mesh=mesh, in_specs=in_specs, out_specs=out_specs, check_vma=False)
```

time: 98.8 us -> 90.9 us (0.920)
  the two profiles are of different devices: /device:TPU:2 before, /device:TPU:48 now
where the time goes in v1:
time: 90.9 us; the launch traced here: 90.6 us
  Pallas kernels  88.4 us (97%)
  local copies, waits for them, and re-layouts  2.26 us (2%)
    pallas_call x1, Pallas kernels, exchange(): pl.pallas_call(exchange_kernel, out_shape=jax.ShapeDtypeStruct((DATES, 51...  88.4 us
    unnamed x1, local copies, waits for them, and re-layouts  2.26 us

profile of v1, /device:TPU:48, one launch (start us, length us, event | category | flops | bytes accessed | tf_op | source)
XLA Modules:
  0.0 90.6 jit_solution(6388092319338840660)
XLA Ops:
  0.0 88.4 %exchange.1 = f32[512,512]{1,0:T(8,128)} custom-call(bf16[8192,128]{1,0:T(8,128)(2,1)} %bitcast.5, f32[1,8]{1,0:T(1,128)} %w_ref.1, s32[2,1200]{1,0:T(2,128)} %bitcast.6, s32[2,1200]{1,0:T(2,128)} %bitcast.7, s32[1,64]{1,0:T(1,128)} %numbers_ref.1, s32[4,64]{1,0:T(4,128)} %bitcast.8), custom_call_target="tpu_custom_call" | custom-call | tf_op jit(solution)/shard_map/exchange/pallas_call | solution.py:592
  88.4 2.3 %copy.7 = f32[512,512]{1,0:T(8,128)} copy(f32[512,512]{1,0:T(8,128)} %exchange.1) | data formatting | bytes 2097152

commit v2 on v1

--- a/solution.py
+++ b/solution.py
@@ -19,7 +19,7 @@
 N_PIX = 8
 CHUNK = 8
 BATCH = 40
-EARLY_LEVELS = 3
+EARLY_LEVELS = 4
 VMEM_BYTES = 56 * 1024 * 1024
 MESH = pl.DeviceIdType.MESH
 f32 = jnp.float32
@@ -54,7 +54,7 @@
             ).astype(bf16)
 
 
-def resample_chunk(at, pick, x_ref, e_ref, spread_ref, o_ref):
+def resample_chunk(at, to, pick, x_ref, e_ref, spread_ref, o_ref):
     parts = []
     for k in range(CHUNK):
         rows = pl.ds(pl.multiple_of((at * CHUNK + k) * 128, 128), 128)
@@ -64,7 +64,7 @@
     for j in range(LOOKS):
         spread_ref[pl.ds(j, CHUNK * 32, stride=LOOKS), :] = y[:, j * 128 : (j + 1) * 128]
     for k in range(CHUNK // 2):
-        o_ref[at * (CHUNK // 2) + k] = (
+        o_ref[to * (CHUNK // 2) + k] = (
             spread_ref[k * 256 : (k + 1) * 256, :].astype(bf16).reshape(2, 8, 16, 128)
         )
 
@@ -245,7 +245,7 @@
 
 def place_group(slot, pix, parity, part, landed_ref, codes_ref, stack_ref, swapped_ref):
     half = iota((128, 128), 1) < 64
-    blocks = landed_ref[part * 8 : (part + 1) * 8, parity, pix].reshape(128, 128)
+    blocks = landed_ref[pl.ds(part * 8, 8), parity, pix].reshape(128, 128)
     row = codes_ref[pix, pl.ds(parity * 4 + part, 1), :]
     chooser = jnp.where(slot == row, 1.0, 0.0).astype(bf16)
     turned = pltpu.roll(blocks.astype(f32), 64, 1)
@@ -321,156 +321,89 @@
 
     pl.semaphore_wait(barrier, N_PIX - 1 + HALF_TILES - 1 + HALF_TILES)
 
-    def pix_first(step):
+    def remote(src, dst, send, recv, device):
+        return pltpu.make_async_remote_copy(
+            src_ref=src, dst_ref=dst, send_sem=send, recv_sem=recv,
+            device_id=device, device_id_type=MESH,
+        )
+
+    row = lax.div(u, 4)
+
+    def pix_first(step, first):
         to = z_of(step)
-        return pltpu.make_async_remote_copy(
-            src_ref=o_ref.at[:, core, to], dst_ref=z_mid.at[z],
-            send_sem=send_z1.at[step], recv_sem=recv_z1.at[step],
-            device_id=(a, to), device_id_type=MESH,
-        )
-
-    def pix_first_part(step, at):
-        to = z_of(step)
-        tiles = pl.ds(at * 4, 4)
-        return pltpu.make_async_remote_copy(
-            src_ref=o_ref.at[tiles, core, to], dst_ref=z_mid.at[z, tiles],
-            send_sem=send_z1.at[step], recv_sem=recv_z1.at[step],
-            device_id=(a, to), device_id_type=MESH,
-        )
-
-    def tile_near(down, across):
-        return lax.rem(lax.div(u, 4) + down, 8) * 4 + lax.rem(u + across, 4)
-
-    def date_first(down, across):
-        to = tile_near(down, across)
-        return pltpu.make_async_remote_copy(
-            src_ref=o_ref.at[to, other], dst_ref=d_mid.at[u],
-            send_sem=send_d1.at[down * 4 + across], recv_sem=recv_d1.at[down * 4 + across],
-            device_id=(2 * to + other, z), device_id_type=MESH,
+        tiles = slice(first, first + 16)
+        return remote(
+            o_ref.at[tiles, core, to], z_mid.at[z, tiles],
+            send_z1.at[0], recv_z1.at[0], (a, to),
+        )
+
+    def date_first(place, across):
+        x = lax.rem(u + across, 4)
+        to = lax.rem(row + place + 2, 8) * 4 + x
+        return remote(
+            o_ref.at[place * 4 + x, other], d_mid.at[u],
+            send_d1.at[0], recv_d1.at[0], (2 * to + other, z),
         )
 
     def date_second(step):
-        to = u_of(step)
-        return pltpu.make_async_remote_copy(
-            src_ref=z_mid.at[:, to], dst_ref=landed_ref.at[u, core],
-            send_sem=send_d2.at[step], recv_sem=recv_d2.at[step],
-            device_id=(2 * to + core, z), device_id_type=MESH,
+        place = lax.div(step, 4)
+        x = lax.rem(u + step, 4)
+        to = lax.rem(row + place + 2, 8) * 4 + x
+        return remote(
+            z_mid.at[:, place * 4 + x], landed_ref.at[u, core],
+            send_d2.at[0], recv_d2.at[lax.div(u, 8)], (2 * to + core, z),
         )
 
     def pix_second(step):
         to = z_of(step)
-        return pltpu.make_async_remote_copy(
-            src_ref=d_mid.at[:, to], dst_ref=landed_ref.at[:, other, z],
-            send_sem=send_z2.at[step], recv_sem=recv_z2.at[step],
-            device_id=(a, to), device_id_type=MESH,
-        )
-
-    def arrival_pix_first(step):
-        at = lax.rem(z + N_PIX - step, N_PIX)
-        return pltpu.make_async_remote_copy(
-            src_ref=o_ref.at[:, core, at], dst_ref=z_mid.at[at],
-            send_sem=send_z1.at[step], recv_sem=recv_z1.at[step],
-            device_id=(a, at), device_id_type=MESH,
-        )
-
-    def arrival_date_first(step):
-        down = lax.div(step, 4)
-        across = lax.rem(step, 4)
-        at = tile_near(8 - down, 4 - across)
-        return pltpu.make_async_remote_copy(
-            src_ref=o_ref.at[at, other], dst_ref=d_mid.at[at],
-            send_sem=send_d1.at[step], recv_sem=recv_d1.at[step],
-            device_id=(2 * at + other, z), device_id_type=MESH,
-        )
-
-    def arrival_date_second(step):
-        at = lax.rem(u + HALF_TILES - step, HALF_TILES)
-        return pltpu.make_async_remote_copy(
-            src_ref=z_mid.at[:, at], dst_ref=landed_ref.at[at, core],
-            send_sem=send_d2.at[step], recv_sem=recv_d2.at[step],
-            device_id=(2 * at + core, z), device_id_type=MESH,
-        )
-
-    def arrival_pix_second(step):
-        at = lax.rem(z + N_PIX - step, N_PIX)
-        return pltpu.make_async_remote_copy(
-            src_ref=d_mid.at[:, at], dst_ref=landed_ref.at[:, other, at],
-            send_sem=send_z2.at[step], recv_sem=recv_z2.at[step],
-            device_id=(a, at), device_id_type=MESH,
-        )
-
-    def code_to_other(step):
-        to = 2 * u_of(step) + other
-        return pltpu.make_async_remote_copy(
-            src_ref=own_codes_ref.at[to], dst_ref=c_mid.at[a],
-            send_sem=send_c1.at[step], recv_sem=recv_c1.at[step],
-            device_id=(to, z), device_id_type=MESH,
-        )
-
-    def code_to_same(step):
-        to = 2 * u_of(step) + core
-        return pltpu.make_async_remote_copy(
-            src_ref=own_codes_ref.at[to], dst_ref=c_mid.at[a],
-            send_sem=send_c1.at[HALF_TILES + step], recv_sem=recv_c1.at[HALF_TILES + step],
-            device_id=(to, z), device_id_type=MESH,
-        )
-
-    def arrival_code_other(step):
-        at = 2 * lax.rem(u + HALF_TILES - step, HALF_TILES) + other
-        return pltpu.make_async_remote_copy(
-            src_ref=own_codes_ref.at[at], dst_ref=c_mid.at[at],
-            send_sem=send_c1.at[step], recv_sem=recv_c1.at[step],
-            device_id=(at, z), device_id_type=MESH,
-        )
-
-    def arrival_code_same(step):
-        at = 2 * lax.rem(u + HALF_TILES - step, HALF_TILES) + core
-        return pltpu.make_async_remote_copy(
-            src_ref=own_codes_ref.at[at], dst_ref=c_mid.at[at],
-            send_sem=send_c1.at[HALF_TILES + step], recv_sem=recv_c1.at[HALF_TILES + step],
-            device_id=(at, z), device_id_type=MESH,
+        return remote(
+            d_mid.at[:, to], landed_ref.at[:, other, z],
+            send_z2.at[0], recv_z2.at[step], (a, to),
+        )
+
+    def code_first(step, parity):
+        to = 2 * u_of(step) + parity
+        return remote(
+            own_codes_ref.at[to], c_mid.at[a], send_c1.at[0], recv_c1.at[0], (to, z)
         )
 
     def code_second(step):
-        to = z_of(step)
-        return pltpu.make_async_remote_copy(
-            src_ref=c_sum, dst_ref=c_all.at[z],
-            send_sem=send_c2.at[step], recv_sem=recv_c2.at[step],
-            device_id=(a, to), device_id_type=MESH,
-        )
-
-    def arrival_code_second(step):
-        at = lax.rem(z + N_PIX - step, N_PIX)
-        return pltpu.make_async_remote_copy(
-            src_ref=c_sum, dst_ref=c_all.at[at],
-            send_sem=send_c2.at[step], recv_sem=recv_c2.at[step],
-            device_id=(a, at), device_id_type=MESH,
-        )
+        return remote(
+            c_sum, c_all.at[z], send_c2.at[0], recv_c2.at[step], (a, z_of(step))
+        )
+
+    def arrived(ref, sem):
+        remote(ref, ref, sem, sem, (a, z_of(1))).wait_recv()
+
+    def departed(ref, sem):
+        remote(ref, ref, sem, sem, (a, z_of(1))).wait_send()
 
     pick = row_picker()
 
     def send_chunk(step):
         down = chunk_of(step)
-        at = lax.rem(lax.div(u, 4) + down, 8)
+        place = lax.rem(down + 6, 8)
         load_chunk(step).wait()
-        resample_chunk(at, pick, x_ref, e_ref, spread_ref, o_ref)
+        resample_chunk(
+            lax.rem(row + down, 8), place, pick, x_ref, e_ref, spread_ref, o_ref
+        )
         for across in range(4):
-            date_first(down, across).start()
-        each(1, N_PIX, lambda s: pix_first_part(s, at).start())
-
-    each(0, 8, send_chunk)
-    own_first = pltpu.make_async_copy(o_ref.at[:, core, z], z_mid.at[z], local_sem.at[0])
-    own_first.start()
-    each(0, HALF_TILES, lambda s: code_to_other(s).start())
-    each(1, HALF_TILES, lambda s: code_to_same(s).start())
-    c_mid[a] = own_codes_ref[a]
+            date_first(place, across).start()
+
+    each(0, 4, send_chunk)
+    each(1, N_PIX, lambda s: pix_first(s, 0).start())
+    each(4, 8, send_chunk)
+    each(1, N_PIX, lambda s: pix_first(s, 16).start())
+    pltpu.make_async_copy(o_ref.at[:, core, z], z_mid.at[z], recv_z1.at[0]).start()
+    each(0, HALF_TILES, lambda s: code_first(s, other).start())
+    each(1, HALF_TILES, lambda s: code_first(s, core).start())
+    pltpu.make_async_copy(own_codes_ref.at[a], c_mid.at[a], recv_c1.at[0]).start()
 
     parts = normal_parts(couples_ref, design_ref)
     parts = reduce_level(0, parts, left_ref)
     parts = reduce_levels(parts, left_ref, factor_ref, 1, EARLY_LEVELS)
 
-    each(0, HALF_TILES, lambda s: arrival_code_other(s).wait_recv())
-    each(1, HALF_TILES, lambda s: arrival_code_same(s).wait_recv())
+    arrived(c_mid, recv_c1.at[0])
     for e in range(2):
         for p in range(4):
             total = c_mid[16 * p + e]
@@ -480,54 +413,58 @@
     c_all[z] = c_sum[...]
     each(1, N_PIX, lambda s: code_second(s).start())
 
-    own_first.wait()
-    each(1, N_PIX, lambda s: arrival_pix_first(s).wait_recv())
-    each(1, HALF_TILES, lambda s: date_second(s).start())
-    own_date = pltpu.make_async_copy(
-        z_mid.at[:, u], landed_ref.at[u, core], local_sem.at[1]
-    )
-    own_date.start()
-    each(0, HALF_TILES, lambda s: arrival_date_first(s).wait_recv())
+    arrived(z_mid, recv_z1.at[0])
+    each(0, 24, lambda s: date_second(s).start())
+    each(25, 32, lambda s: date_second(s).start())
+    pltpu.make_async_copy(
+        z_mid.at[:, 24 + lax.rem(u, 4)], landed_ref.at[u, core], recv_d2.at[lax.div(u, 8)]
+    ).start()
+    arrived(d_mid, recv_d1.at[0])
     each(1, N_PIX, lambda s: pix_second(s).start())
     own_pix = pltpu.make_async_copy(
-        d_mid.at[:, z], landed_ref.at[:, other, z], local_sem.at[2]
+        d_mid.at[:, z], landed_ref.at[:, other, z], local_sem.at[0]
     )
     own_pix.start()
 
     parts = reduce_levels(parts, left_ref, factor_ref, EARLY_LEVELS, 6)
     finish_operator(parts, left_ref, factor_ref, terms_ref, design_ref, high_ref, low_ref)
 
-    each(1, N_PIX, lambda s: arrival_code_second(s).wait_recv())
-
-    row = iota((256, 128), 0)
+    each(1, N_PIX, lambda s: arrived(c_sum, recv_c2.at[s]))
+
+    line = iota((256, 128), 0)
     column = iota((256, 128), 1)
-    fits = (row // 32 == column // 16) & (row // 8 % 4 == column % 4)
-    slot = jnp.where(fits, row % 8, -1).astype(f32)
-
-    def place_pix(pix, parity):
+    fits = (line // 32 == column // 16) & (line // 8 % 4 == column % 4)
+    slot = jnp.where(fits, line % 8, -1).astype(f32)
+
+    def place(pix, parity, part):
+        place_group(slot, pix, parity, part, landed_ref, c_all, stack_ref, swapped_ref)
+
+    def land_pix(step):
+        at = lax.rem(z + N_PIX - step, N_PIX)
+        arrived(landed_ref.at[:, other, at], recv_z2.at[step])
         for part in range(4):
-            place_group(slot, pix, parity, part, landed_ref, c_all, stack_ref, swapped_ref)
-
-    def land_pix(step):
-        arrival_pix_second(step).wait_recv()
-        place_pix(lax.rem(z + N_PIX - step, N_PIX), other)
+            place(at, other, part)
+
+    def land_dates(step):
+        part = lax.rem(lax.div(u, 8) + 2 + step, 4)
+        arrived(landed_ref.at[pl.ds(part * 8, 8), core], recv_d2.at[part])
+        for pix in range(N_PIX):
+            place(pix, core, part)
 
     own_pix.wait()
-    place_pix(z, other)
+    for part in range(4):
+        place(z, other, part)
     each(1, N_PIX, land_pix)
-    own_date.wait()
-    each(1, HALF_TILES, lambda s: arrival_date_second(s).wait_recv())
-    each(0, N_PIX, lambda pix: place_pix(pix, core))
+    each(0, 4, land_dates)
 
     solve_phases(pairs_ref, high_ref, low_ref, out_ref, stack_ref, swapped_ref, phase_ref)
 
-    each(0, HALF_TILES, lambda s: code_to_other(s).wait_send())
-    each(1, HALF_TILES, lambda s: code_to_same(s).wait_send())
-    each(1, N_PIX, lambda s: code_second(s).wait_send())
-    each(1, N_PIX, lambda s: pix_first(s).wait_send())
-    each(0, HALF_TILES, lambda s: date_first(lax.div(s, 4), lax.rem(s, 4)).wait_send())
-    each(1, HALF_TILES, lambda s: date_second(s).wait_send())
-    each(1, N_PIX, lambda s: pix_second(s).wait_send())
+    departed(own_codes_ref.at[0 : TILES - 1], send_c1.at[0])
+    departed(c_all.at[0 : N_PIX - 1], send_c2.at[0])
+    departed(o_ref.at[:, 0, 0 : N_PIX - 1], send_z1.at[0])
+    departed(o_ref.at[:, 0], send_d1.at[0])
+    departed(z_mid.at[:, 0 : HALF_TILES - 1], send_d2.at[0])
+    departed(d_mid.at[:, 0 : N_PIX - 1], send_z2.at[0])
 
 
 def solve_phases(pairs_ref, high_ref, low_ref, out_ref, stack_ref, swapped_ref, phase_ref):
@@ -615,13 +552,13 @@
             pltpu.VMEM((DATES, DATES), f32),
             pltpu.VMEM((DATES, DATES), f32),
             pltpu.VMEM((3, DATES, DATES), bf16),
-            dma((N_PIX,)), dma((N_PIX,)),
-            dma((HALF_TILES,)), dma((HALF_TILES,)),
-            dma((HALF_TILES,)), dma((HALF_TILES,)),
-            dma((N_PIX,)), dma((N_PIX,)),
-            dma((3,)), dma((8,)),
-            dma((2 * HALF_TILES,)), dma((2 * HALF_TILES,)),
-            dma((N_PIX,)), dma((N_PIX,)),
+            dma((1,)), dma((1,)),
+            dma((1,)), dma((1,)),
+            dma((1,)), dma((4,)),
+            dma((1,)), dma((N_PIX,)),
+            dma((1,)), dma((8,)),
+            dma((1,)), dma((1,)),
+            dma((1,)), dma((N_PIX,)),
         ],
         compiler_params=pltpu.CompilerParams(
             collective_id=0, has_side_effects=True, vmem_limit_bytes=VMEM_BYTES

time: 90.9 us -> 86.1 us (0.947)
  the two profiles are of different devices: /device:TPU:48 before, /device:TPU:32 now
where the time goes in v2:
time: 86.1 us; the launch traced here: 85.9 us
  Pallas kernels  83.6 us (97%)
  local copies, waits for them, and re-layouts  2.26 us (3%)
    pallas_call x1, Pallas kernels, exchange(): pl.pallas_call(exchange_kernel, out_shape=jax.ShapeDtypeStruct((DATES, 51...  83.6 us
    unnamed x1, local copies, waits for them, and re-layouts  2.26 us

profile of v2, /device:TPU:32, one launch (start us, length us, event | category | flops | bytes accessed | tf_op | source)
XLA Modules:
  0.0 85.9 jit_solution(18431914998870801774)
XLA Ops:
  0.0 83.6 %exchange.1 = f32[512,512]{1,0:T(8,128)} custom-call(bf16[8192,128]{1,0:T(8,128)(2,1)} %bitcast.5, f32[1,8]{1,0:T(1,128)} %w_ref.1, s32[2,1200]{1,0:T(2,128)} %bitcast.6, s32[2,1200]{1,0:T(2,128)} %bitcast.7, s32[1,64]{1,0:T(1,128)} %numbers_ref.1, s32[4,64]{1,0:T(4,128)} %bitcast.8), custom_call_target="tpu_custom_call" | custom-call | tf_op jit(solution)/shard_map/exchange/pallas_call | solution.py:529
  83.6 2.3 %copy.7 = f32[512,512]{1,0:T(8,128)} copy(f32[512,512]{1,0:T(8,128)} %exchange.1) | data formatting | bytes 2097152

commit v3 on v2

--- a/solution.py
+++ b/solution.py
@@ -319,8 +319,6 @@
     build_row_matrix(w_ref, e_ref)
     own_code_rows(u, numbers_ref, places_ref, own_codes_ref)
 
-    pl.semaphore_wait(barrier, N_PIX - 1 + HALF_TILES - 1 + HALF_TILES)
-
     def remote(src, dst, send, recv, device):
         return pltpu.make_async_remote_copy(
             src_ref=src, dst_ref=dst, send_sem=send, recv_sem=recv,
@@ -329,16 +327,15 @@
 
     row = lax.div(u, 4)
 
-    def pix_first(step, first):
+    def pix_first(step):
         to = z_of(step)
-        tiles = slice(first, first + 16)
         return remote(
-            o_ref.at[tiles, core, to], z_mid.at[z, tiles],
-            send_z1.at[0], recv_z1.at[0], (a, to),
-        )
-
-    def date_first(place, across):
-        x = lax.rem(u + across, 4)
+            o_ref.at[:, core, to], z_mid.at[z], send_z1.at[0], recv_z1.at[0], (a, to)
+        )
+
+    def date_first(step):
+        place = lax.div(step, 4)
+        x = lax.rem(u + step, 4)
         to = lax.rem(row + place + 2, 8) * 4 + x
         return remote(
             o_ref.at[place * 4 + x, other], d_mid.at[u],
@@ -380,20 +377,18 @@
 
     pick = row_picker()
 
-    def send_chunk(step):
+    def ready_chunk(step):
         down = chunk_of(step)
         place = lax.rem(down + 6, 8)
         load_chunk(step).wait()
         resample_chunk(
             lax.rem(row + down, 8), place, pick, x_ref, e_ref, spread_ref, o_ref
         )
-        for across in range(4):
-            date_first(place, across).start()
-
-    each(0, 4, send_chunk)
-    each(1, N_PIX, lambda s: pix_first(s, 0).start())
-    each(4, 8, send_chunk)
-    each(1, N_PIX, lambda s: pix_first(s, 16).start())
+
+    each(0, 8, ready_chunk)
+    pl.semaphore_wait(barrier, N_PIX - 1 + HALF_TILES - 1 + HALF_TILES)
+    each(1, N_PIX, lambda s: pix_first(s).start())
+    each(0, HALF_TILES, lambda s: date_first(s).start())
     pltpu.make_async_copy(o_ref.at[:, core, z], z_mid.at[z], recv_z1.at[0]).start()
     each(0, HALF_TILES, lambda s: code_first(s, other).start())
     each(1, HALF_TILES, lambda s: code_first(s, core).start())

time: 86.1 us -> 88 us (1.022)
  the two profiles are of different devices: /device:TPU:32 before, /device:TPU:8 now
where the time goes in v3:
time: 88 us; the launch traced here: 87.7 us
  Pallas kernels  85.5 us (97%)
  local copies, waits for them, and re-layouts  2.26 us (3%)
    pallas_call x1, Pallas kernels, exchange(): pl.pallas_call(exchange_kernel, out_shape=jax.ShapeDtypeStruct((DATES, 51...  85.5 us
    unnamed x1, local copies, waits for them, and re-layouts  2.26 us

profile of v3, /device:TPU:8, one launch (start us, length us, event | category | flops | bytes accessed | tf_op | source)
XLA Modules:
  0.0 87.7 jit_solution(5432227532084519777)
XLA Ops:
  0.0 85.5 %exchange.1 = f32[512,512]{1,0:T(8,128)} custom-call(bf16[8192,128]{1,0:T(8,128)(2,1)} %bitcast.5, f32[1,8]{1,0:T(1,128)} %w_ref.1, s32[2,1200]{1,0:T(2,128)} %bitcast.6, s32[2,1200]{1,0:T(2,128)} %bitcast.7, s32[1,64]{1,0:T(1,128)} %numbers_ref.1, s32[4,64]{1,0:T(4,128)} %bitcast.8), custom_call_target="tpu_custom_call" | custom-call | tf_op jit(solution)/shard_map/exchange/pallas_call | solution.py:524
  85.5 2.3 %copy.7 = f32[512,512]{1,0:T(8,128)} copy(f32[512,512]{1,0:T(8,128)} %exchange.1) | data formatting | bytes 2097152
